TPU v7x, 32 devices: a whole 2x2x4 slice. The times are simulated.
32 devices in a mesh: group: 2 (over x), pos: 16 (over z, y, core).
Axes of the slice: x: 2, y: 2, z: 4, core: 2. Of those that a mesh axis runs over, the one named last changes fastest.
Arguments:
- acts: bfloat16 [4, 1024, 1536], P('group', 'pos'), parts along dimension 0, may hold values from -12 to 12
- skips: bfloat16 [4, 2048, 1280], P('group', 'pos'), parts along dimension 0, may hold values from -6 to 6
- norm_gain: float32 [1536], replicated, may hold values from 0.6 to 1.6
- w_query: bfloat16 [1536, 256], replicated, may hold values from -4 to 4
- w_key: bfloat16 [1536, 256], replicated, may hold values from -4 to 4
- w_value: bfloat16 [1536, 768], replicated, may hold values from -0.15625 to 0.15625
- w_out: bfloat16 [768, 1536], replicated, may hold values from -0.21875 to 0.21875
- w_lift: bfloat16 [1536, 1536], P('pos'), may hold values from -0.15625 to 0.15625
- w_skip: bfloat16 [1280, 1536], P('pos'), may hold values from -0.15625 to 0.15625
- depth_kernel: float32 [3, 1536], replicated, may hold values from -3 to 3
- w_point: bfloat16 [1536, 1536], P(None, 'pos'), may hold values from -0.15625 to 0.15625
Outputs:
- decoded: bfloat16 [4, 2048, 1536], P('group', 'pos'), parts along dimension 0
There are 2 independent parts, one for each index of `group`. A program takes and returns all parts, laid end to end along the dimension named above; an argument that names none is the same for every part. Nothing has to cross between parts.
All inputs are finite; a program needn't handle non-finite values.
Results may differ from a plain program's by a relative error of at most 0.014.
Values may be sent and summed in bfloat16 or wider, within the bound.
A program may use at most 128 MiB of HBM per device.

v0:
```python
import jax
import jax.numpy as jnp
from jax import lax
from jax.sharding import PartitionSpec as P

HEADS = 4
HK = 64
HV = 192


def extended(cells, sides, width):
    for axis, dim in sides:
        count = lax.axis_size(axis)
        ends = count - 1
        head = lax.slice_in_dim(cells, 0, width, axis=dim)
        tail = lax.slice_in_dim(cells, cells.shape[dim] - width, cells.shape[dim], axis=dim)
        cells = jnp.concatenate(
            [
                lax.ppermute(tail, axis, [(i, (i + 1) % count) for i in range(ends)]),
                cells,
                lax.ppermute(head, axis, [((i + 1) % count, i) for i in range(ends)]),
            ],
            axis=dim,
        )
    return cells


def on_device(
    acts, skips, norm_gain, w_query, w_key, w_value, w_out, w_lift, w_skip, depth_kernel, w_point
):
    lift_full, skip_full, point_full = (
        lax.all_gather(w_lift, "pos", axis=0, tiled=True),
        lax.all_gather(w_skip, "pos", axis=0, tiled=True),
        lax.all_gather(w_point, "pos", axis=1, tiled=True),
    )
    seq_count, bin_rows, width = acts.shape
    actsf = acts.astype(jnp.float32)
    centre = actsf - jnp.mean(actsf, axis=-1, keepdims=True)
    normed = (
        centre * lax.rsqrt(jnp.mean(centre * centre, axis=-1, keepdims=True) + 1e-05) * norm_gain
    ).astype(jnp.bfloat16)
    flat = normed.reshape(seq_count * bin_rows, width)
    queries = (
        (jnp.dot(flat, w_query, preferred_element_type=jnp.float32) * HK ** (-0.5))
        .astype(jnp.bfloat16)
        .reshape(seq_count, bin_rows, HEADS, HK)
    )
    keys_here = (
        jnp.dot(flat, w_key, preferred_element_type=jnp.float32)
        .astype(jnp.bfloat16)
        .reshape(seq_count, bin_rows, HEADS * HK)
    )
    values_here = (
        jnp.dot(flat, w_value, preferred_element_type=jnp.float32)
        .astype(jnp.bfloat16)
        .reshape(seq_count, bin_rows, HEADS * HV)
    )
    running = jnp.full((seq_count, HEADS, bin_rows), -1e30, jnp.float32)
    key_piece = lax.all_gather(keys_here, "pos", axis=1, tiled=True)
    value_piece = lax.all_gather(values_here, "pos", axis=1, tiled=True)
    count = key_piece.shape[1]
    keyed = key_piece.reshape(seq_count, count, HEADS, HK)
    valued = value_piece.reshape(seq_count, count, HEADS, HV)
    scores = jnp.einsum("sqhd,skhd->shqk", queries, keyed, preferred_element_type=jnp.float32)
    newest = jnp.maximum(running, jnp.max(scores, axis=-1))
    weights = jnp.exp(scores - newest[..., None])
    totals = jnp.sum(weights, axis=-1)
    summed = jnp.einsum(
        "shqk,skhv->shqv", weights.astype(jnp.bfloat16), valued, preferred_element_type=jnp.float32
    )
    running, totals, summed = (newest, totals, summed)
    mixed = (
        (summed / totals[..., None])
        .transpose(0, 2, 1, 3)
        .reshape(seq_count * bin_rows, HEADS * HV)
        .astype(jnp.bfloat16)
    )
    attended = (
        actsf.reshape(seq_count * bin_rows, width)
        + jnp.dot(mixed, w_out, preferred_element_type=jnp.float32)
    ).astype(jnp.bfloat16)
    activated = jax.nn.gelu(attended.astype(jnp.float32)).astype(jnp.bfloat16)
    lifted = jnp.dot(activated, lift_full, preferred_element_type=jnp.float32)
    lifted = lifted.astype(jnp.bfloat16).reshape(seq_count, bin_rows, width)
    raised = jnp.repeat(lifted, 2, axis=1).reshape(seq_count * 2 * bin_rows, width)
    skip_act = (
        jax.nn.gelu(skips.astype(jnp.float32))
        .astype(jnp.bfloat16)
        .reshape(seq_count * 2 * bin_rows, skips.shape[2])
    )
    skip_term = jnp.dot(skip_act, skip_full, preferred_element_type=jnp.float32)
    merged = (
        (raised.astype(jnp.float32) + skip_term)
        .astype(jnp.bfloat16)
        .reshape(seq_count, 2 * bin_rows, width)
    )
    padded = extended(merged, (("pos", 1),), 1)
    paddedf = padded.astype(jnp.float32)
    spread = (
        depth_kernel[0] * paddedf[:, :-2]
        + depth_kernel[1] * paddedf[:, 1:-1]
        + depth_kernel[2] * paddedf[:, 2:]
    ).astype(jnp.bfloat16)
    spread = spread.reshape(seq_count * 2 * bin_rows, width)
    decoded = jnp.dot(spread, point_full, preferred_element_type=jnp.float32)
    return decoded.astype(jnp.bfloat16).reshape(seq_count, 2 * bin_rows, width)


def solution(mesh):
    return jax.shard_map(
        on_device,
        mesh=mesh,
        in_specs=(
            P("group", "pos", None),
            P("group", "pos", None),
            P(),
            P(),
            P(),
            P(),
            P(),
            P("pos", None),
            P("pos", None),
            P(),
            P(None, "pos"),
        ),
        out_specs=P("group", "pos", None),
        check_vma=False,
    )
```

profile of v0, /device:TPU:0, one launch (start us, length us, event | category | flops | bytes accessed | tf_op | source)
XLA Modules:
  0.0 268.4 jit_solution(8063212985456525454)
XLA Ops:
  6.5 1.3 convert_reduce_fusion
  7.8 1.3 multiply_reduce_fusion
  9.1 1.3 multiply_convert_fusion
  10.4 0.9 convolution_convert_fusion.3
  11.4 2.9 %convolution_convert_fusion.2 = bf16[128,768]{1,0:T(8,128)(2,1)} fusion(bf16[128,1536]{1,0:T(8,128)(2,1)S(1)} %bitcast.36, bf16[1536,768]{1,0:T(8,128)(2,1)} %param.16), kind=kOutput, calls=%fused_computation.30 | convolution fusion | flops 302088192 | bytes 2949120 | tf_op jit(solution)/shard_map/dot_general | solution.py:54
  14.3 0.7 all-gather.10.cloned.1.call-update
  15.1 0.5 all-gather.12.cloned.1.call-update
  15.6 0.5 all-gather.14.cloned.1.call-update
  16.2 0.9 fusion.16
  17.1 1.0 reshape.61
  18.1 2.4 fusion.13
  20.4 31.7 %all-gather.6.cloned.1.call-done = bf16[2,1024,256]{2,1,0:T(8,128)(2,1)} async-done(((bf16[2,64,256]{2,1,0:T(8,128)(2,1)}), bf16[2,1024,256]{2,1,0:T(8,128)(2,1)}) %all-gather.6.cloned.1.call-update) | async-done | bytes 1048592 | tf_op jit(solution)/shard_map/all_gather | solution.py:59
  52.1 1.5 copy.15
  53.6 0.5 fusion.38
  54.1 1.3 copy-done.1
  55.5 0.5 fusion.3
  56.0 42.6 %all-gather.8.cloned.1.call-done = bf16[2,1024,768]{2,1,0:T(8,128)(2,1)} async-done(((bf16[2,64,768]{2,1,0:T(8,128)(2,1)}), bf16[2,1024,768]{2,1,0:T(8,128)(2,1)}) %all-gather.8.cloned.1.call-update) | async-done | bytes 3145744 | tf_op jit(solution)/shard_map/all_gather | solution.py:60
  98.6 4.6 %copy.17 = bf16[2,1024,768]{1,2,0:T(8,128)(2,1)} copy(bf16[2,1024,768]{2,1,0:T(8,128)(2,1)} %all-gather.8.cloned.1.call-done) | data formatting | bytes 6291456 | tf_op jit(solution)/shard_map/all_gather | solution.py:60
  103.2 3.7 %fusion.15 = bf16[2,64,4,192]{3,1,2,0:T(8,128)(2,1)S(1)} fusion(bf16[2,1024,4,192]{1,3,2,0:T(8,128)(2,1)} %bitcast.40, f32[2,4,64,1024]{3,2,1,0:T(8,128)} %copy-done.1, f32[2,4,64]{2,1,0:T(4,128)S(1)} %broadcast_maximum_fusion, f32[2,64,4]{1,2,0:T(4,128)S(1)} %bitcast.48), kind=kOutput, calls=%fused_computation.28 | convolution fusion | flops 202571776 | bytes 5443584 | tf_op jit(solution)/shard_map/shqk,skhv->shqv/dot_general | solution.py:68
  107.4 45.7 %all-gather.10.cloned.1.call-done = bf16[1536,1536]{1,0:T(8,128)(2,1)} async-done(((bf16[96,1536]{1,0:T(8,128)(2,1)}), bf16[1536,1536]{1,0:T(8,128)(2,1)}) %all-gather.10.cloned.1.call-update) | async-done | bytes 4718608 | tf_op jit(solution)/shard_map/all_gather | solution.py:32
  153.1 3.7 %convolution_convert_fusion.1 = bf16[128,1536]{1,0:T(8,128)(2,1)S(1)} fusion(bf16[1536,1536]{1,0:T(8,128)(2,1)} %all-gather.10.cloned.1.call-done, bf16[128,768]{1,0:T(8,128)(2,1)S(1)} %convert_element_type.71, bf16[768,1536]{1,0:T(8,128)(2,1)S(1)} %copy-done, bf16[128,1536]{1,0:T(8,128)(2,1)S(1)} %bitcast.39), kind=kOutput, calls=%fused_computation.6 | convolution fusion | flops 908722176 | bytes 8060928 | tf_op jit(solution)/shard_map/dot_general | solution.py:83
  156.8 1.6 broadcast_in_dim.5
  158.3 3.2 %convert_element_type.78 = f32[256,1536]{1,0:T(8,128)} reshape(f32[2,64,2,1536]{3,2,1,0:T(2,128)} %broadcast_in_dim.5) | data formatting | bytes 3145728 | tf_op jit(solution)/shard_map/convert_element_type | solution.py:93
  161.5 41.0 %all-gather.12.cloned.1.call-done = bf16[1280,1536]{1,0:T(8,128)(2,1)} async-done(((bf16[80,1536]{1,0:T(8,128)(2,1)}), bf16[1280,1536]{1,0:T(8,128)(2,1)}) %all-gather.12.cloned.1.call-update) | async-done | bytes 3932176 | tf_op jit(solution)/shard_map/all_gather | solution.py:33
  202.6 3.8 %fusion = bf16[256,1536]{1,0:T(8,128)(2,1)S(1)} fusion(f32[256,1536]{1,0:T(8,128)} %convert_element_type.78, bf16[256,1280]{1,0:T(8,128)(2,1)S(1)} %bitcast.45, bf16[1280,1536]{1,0:T(8,128)(2,1)} %all-gather.12.cloned.1.call-done), kind=kOutput, calls=%fused_computation.1 | convolution fusion | flops 1007419392 | bytes 6946816 | tf_op jit(solution)/shard_map/dot_general | solution.py:91
  206.4 2.2 collective-permute-start
  208.6 1.3 collective-permute-start.1
  210.0 1.7 collective-permute-done.1
  211.7 0.2 maximum_convert_fusion
  211.9 0.5 fusion.6
  212.4 44.8 %all-gather.14.cloned.1.call-done = bf16[1536,1536]{0,1:T(8,128)(2,1)} async-done(((bf16[1536,96]{0,1:T(8,128)(2,1)}), bf16[1536,1536]{0,1:T(8,128)(2,1)}) %all-gather.14.cloned.1.call-update) | async-done | bytes 4718608 | tf_op jit(solution)/shard_map/all_gather | solution.py:34
  257.2 4.6 %convolution_convert_fusion = bf16[256,1536]{1,0:T(8,128)(2,1)} fusion(bf16[256,1536]{1,0:T(8,128)(2,1)S(1)} %bitcast.44, bf16[1536,1536]{0,1:T(8,128)(2,1)} %all-gather.14.cloned.1.call-done), kind=kOutput, calls=%fused_computation.2 | convolution fusion | flops 1208352768 | bytes 6291456 | tf_op jit(solution)/shard_map/dot_general | solution.py:105
  (28 shorter events, 0.8 us)
Async XLA Ops:
  6.5 146.6 %copy-start = (bf16[768,1536]{1,0:T(8,128)(2,1)S(1)}, bf16[768,1536]{1,0:T(8,128)(2,1)}, u32[]{:S(2)}) copy-start(bf16[768,1536]{1,0:T(8,128)(2,1)} %param.17) | copy-start | bytes 7077892
  6.5 3.8 %copy-start.3 = (bf16[1536,256]{1,0:T(8,128)(2,1)S(1)}, bf16[1536,256]{1,0:T(8,128)(2,1)}, u32[]{:S(2)}) copy-start(bf16[1536,256]{1,0:T(8,128)(2,1)} %param.15) | copy-start | bytes 2359300
  6.5 45.6 %all-gather.6.cloned.1.call-start = ((), (), s32[]{:S(2)}) async-start(), calls=%async_computation | async-start | bytes 1114112 | tf_op jit(solution)/shard_map/all_gather | solution.py:59
  11.3 4.9 %copy-start.4 = (bf16[1536,256]{1,0:T(8,128)(2,1)S(1)}, bf16[1536,256]{1,0:T(8,128)(2,1)}, u32[]{:S(2)}) copy-start(bf16[1536,256]{1,0:T(8,128)(2,1)} %param.14) | copy-start | bytes 2359300
  11.3 87.3 %all-gather.8.cloned.1.call-start = ((), (), s32[]{:S(2)}) async-start(), calls=%async_computation.1 | async-start | bytes 3342336 | tf_op jit(solution)/shard_map/all_gather | solution.py:60
  14.3 138.8 %all-gather.10.cloned.1.call-start = ((), (), s32[]{:S(2)}) async-start(), calls=%async_computation.2 | async-start | bytes 5013504 | tf_op jit(solution)/shard_map/all_gather | solution.py:32
  15.0 187.6 %all-gather.12.cloned.1.call-start = ((), (), s32[]{:S(2)}) async-start(), calls=%async_computation.3 | async-start | bytes 4177920 | tf_op jit(solution)/shard_map/all_gather | solution.py:33
  15.6 241.7 %all-gather.14.cloned.1.call-start = ((), (), s32[]{:S(2)}) async-start(), calls=%async_computation.4 | async-start | bytes 5013504 | tf_op jit(solution)/shard_map/all_gather | solution.py:34
  54.1 1.4 copy-start.1
  103.2 49.9 %copy-start.2 = (bf16[2,64,1536]{2,1,0:T(8,128)(2,1)S(1)}, bf16[2,64,1536]{2,1,0:T(8,128)(2,1)}, u32[]{:S(2)}) copy-start(bf16[2,64,1536]{2,1,0:T(8,128)(2,1)} %param.11) | copy-start | bytes 1179652
  158.3 44.3 %copy-start.5 = (bf16[2,128,1280]{2,1,0:T(8,128)(2,1)S(1)}, bf16[2,128,1280]{2,1,0:T(8,128)(2,1)}, u32[]{:S(2)}) copy-start(bf16[2,128,1280]{2,1,0:T(8,128)(2,1)} %fusion.13) | copy-start | bytes 1966084
  202.6 7.3 %copy-start.6 = (f32[3,1536]{1,0:T(4,128)S(1)}, f32[3,1536]{1,0:T(4,128)}, u32[]{:S(2)}) copy-start(f32[3,1536]{1,0:T(4,128)} %param.20) | copy-start | bytes 55300
  206.4 3.5 %collective-permute-start = (bf16[2,1,1536]{2,1,0:T(2,128)(2,1)S(1)}, bf16[2,1,1536]{2,1,0:T(2,128)(2,1)S(1)}, u32[]{:S(2)}, u32[]{:S(2)}) collective-permute-start(bf16[2,1,1536]{2,1,0:T(2,128)(2,1)S(1)} %get-tuple-element.8), channel_id=1, source_target_pairs={{0,1},{1,2},{2,3},{3,4},{4,5},{5,6},{6,7},{7,8},{8,9},{9,10},{10,1... | collective-permute-start | bytes 18440 | tf_op jit(solution)/shard_map/ppermute | solution.py:19
  208.6 3.1 %collective-permute-start.1 = (bf16[2,1,1536]{2,1,0:T(2,128)(2,1)S(1)}, bf16[2,1,1536]{2,1,0:T(2,128)(2,1)S(1)}, u32[]{:S(2)}, u32[]{:S(2)}) collective-permute-start(bf16[2,1,1536]{2,1,0:T(2,128)(2,1)S(1)} %get-tuple-element.9), channel_id=1, source_target_pairs={{1,0},{2,1},{3,2},{4,3},{5,4},{6,5},{7,6},{8,7},{9,8},{10,9},{11,1... | collective-permute-start | bytes 18440 | tf_op jit(solution)/shard_map/ppermute | solution.py:21
Sparse Core Ops, SparseCore 0:
  11.4 40.6 all-gather.5
  54.4 44.1 all-gather.7
  100.9 52.1 all-gather.9
  155.2 47.3 all-gather.11
  204.7 52.4 all-gather.13
where the time goes:
time: 269 us; the launch traced here: 268 us
  waiting for transfers between devices  209 us (78%)
  matrix products  21 us (8%)
  local copies, waits for them, and re-layouts  13.7 us (5%)
  between operations  13.3 us (5%)
  other arithmetic  7.44 us (3%)
  starting transfers between devices  3.61 us (1%)
    all_gather x1, waiting for transfers between devices, on_device(): lax.all_gather(w_lift, 'pos', axis=0, tiled=True)  45.7 us
    all_gather x1, waiting for transfers between devices, on_device(): lax.all_gather(w_point, 'pos', axis=1, tiled=True)  44.8 us
    all_gather x1, waiting for transfers between devices, on_device(): value_piece = lax.all_gather(values_here, 'pos', axis=1, tiled=True)  42.6 us
    all_gather x1, waiting for transfers between devices, on_device(): lax.all_gather(w_skip, 'pos', axis=0, tiled=True)  41 us
    all_gather x1, waiting for transfers between devices, on_device(): key_piece = lax.all_gather(keys_here, 'pos', axis=1, tiled=True)  31.7 us
  transfers between devices with their start and end apart: 7, of which 6 were waited for; matrix products, arithmetic and copies ran while one was open for 12% of the time, Pallas kernels for 0%

commit v1 on v0

--- a/solution.py
+++ b/solution.py
@@ -6,6 +6,18 @@
 HEADS = 4
 HK = 64
 HV = 192
+
+
+def doubled_up(x, axis, dim):
+    ways, here = (lax.axis_size(axis), lax.axis_index(axis))
+    grown, reach = (x, 1)
+    while reach < ways:
+        theirs = lax.ppermute(grown, axis, [(d, d ^ reach) for d in range(ways)])
+        mine_first = jnp.concatenate([grown, theirs], axis=dim)
+        theirs_first = jnp.concatenate([theirs, grown], axis=dim)
+        grown = jnp.where(here & reach == 0, mine_first, theirs_first)
+        reach = 2 * reach
+    return grown
 
 
 def extended(cells, sides, width):
@@ -56,7 +68,7 @@
         .reshape(seq_count, bin_rows, HEADS * HV)
     )
     running = jnp.full((seq_count, HEADS, bin_rows), -1e30, jnp.float32)
-    key_piece = lax.all_gather(keys_here, "pos", axis=1, tiled=True)
+    key_piece = doubled_up(keys_here, "pos", 1)
     value_piece = lax.all_gather(values_here, "pos", axis=1, tiled=True)
     count = key_piece.shape[1]
     keyed = key_piece.reshape(seq_count, count, HEADS, HK)

time: 269 us -> 248 us (0.922)
  waiting for transfers between devices: 209 us -> 174 us
  starting transfers between devices: 3.61 us -> 11.5 us
  other arithmetic: 7.44 us -> 10.7 us
    ppermute x0 -> x4, waiting for transfers between devices: none -> 44.3 us  [doubled_up(): theirs = lax.ppermute(grown, axis, [(d, d ^ reach) for d in range(ways)])]
    all_gather x1, waiting for transfers between devices: 42.6 us -> 0.02 us  [on_device(): value_piece = lax.all_gather(values_here, 'pos', axis=1, tiled=True)]
    all_gather x1 -> x0, waiting for transfers between devices: 31.7 us -> none  [on_device(): key_piece = lax.all_gather(keys_here, 'pos', axis=1, tiled=True)]
    ppermute x0 -> x4, starting transfers between devices: none -> 7.91 us  [doubled_up(): theirs = lax.ppermute(grown, axis, [(d, d ^ reach) for d in range(ways)])]
    all_gather x1, waiting for transfers between devices: 45.7 us -> 40.1 us  [on_device(): lax.all_gather(w_lift, 'pos', axis=0, tiled=True)]
    select_n x0 -> x6, other arithmetic: none -> 3.23 us  [doubled_up(): grown = jnp.where(here & reach == 0, mine_first, theirs_first)]
  transfers between devices with their start and end apart: 7 -> 10, of which waited for: 6 -> 8; matrix products, arithmetic and copies ran while one was open for 12% -> 14% of each run, Pallas kernels for 0% -> 0%
where the time goes in v1:
time: 248 us; the launch traced here: 247 us
  waiting for transfers between devices  174 us (70%)
  matrix products  22.9 us (9%)
  local copies, waits for them, and re-layouts  14.8 us (6%)
  between operations  13.4 us (5%)
  starting transfers between devices  11.5 us (5%)
  other arithmetic  10.7 us (4%)
    all_gather x1, waiting for transfers between devices, on_device(): lax.all_gather(w_point, 'pos', axis=1, tiled=True)  44.9 us
    ppermute x4, waiting for transfers between devices, doubled_up(): theirs = lax.ppermute(grown, axis, [(d, d ^ reach) for d in range(ways)])  44.3 us
    all_gather x1, waiting for transfers between devices, on_device(): lax.all_gather(w_skip, 'pos', axis=0, tiled=True)  41.1 us
    all_gather x1, waiting for transfers between devices, on_device(): lax.all_gather(w_lift, 'pos', axis=0, tiled=True)  40.1 us
    ppermute x4, starting transfers between devices, doubled_up(): theirs = lax.ppermute(grown, axis, [(d, d ^ reach) for d in range(ways)])  7.91 us
  transfers between devices with their start and end apart: 10, of which 8 were waited for; matrix products, arithmetic and copies ran while one was open for 14% of the time, Pallas kernels for 0%

profile of v1, /device:TPU:0, one launch (start us, length us, event | category | flops | bytes accessed | tf_op | source)
XLA Modules:
  0.0 247.2 jit_solution(17950774414102457658)
XLA Ops:
  6.5 1.3 convert_reduce_fusion
  7.8 1.3 multiply_reduce_fusion
  9.1 1.3 multiply_convert_fusion
  10.4 2.9 %convolution_convert_fusion.2 = bf16[128,768]{1,0:T(8,128)(2,1)} fusion(bf16[128,1536]{1,0:T(8,128)(2,1)S(1)} %bitcast.37, bf16[1536,768]{1,0:T(8,128)(2,1)} %param.16), kind=kOutput, calls=%fused_computation.30 | convolution fusion | flops 302088192 | bytes 2949120 | tf_op jit(solution)/shard_map/dot_general | solution.py:66
  16.7 1.1 collective-permute-done
  17.9 1.0 maximum_select_fusion.7
  18.8 2.9 %collective-permute-start.1 = (bf16[2,128,256]{2,1,0:T(8,128)(2,1)S(1)}, bf16[2,128,256]{2,1,0:T(8,128)(2,1)S(1)}, u32[]{:S(2)}, u32[]{:S(2)}) collective-permute-start(bf16[2,128,256]{2,1,0:T(8,128)(2,1)S(1)} %maximum_select_fusion.7), channel_id=1, source_target_pairs={{0,2},{1,3},{2,0},{3,1},{4,6},{5,7},{6,4},{7,5},{8,10},{9,11},{10,... | collective-permute-start | bytes 393224 | tf_op jit(solution)/shard_map/ppermute | solution.py:15
  21.7 1.0 concatenate.57
  22.9 2.7 %collective-permute-done.1 = bf16[2,128,256]{2,1,0:T(8,128)(2,1)S(1)} collective-permute-done((bf16[2,128,256]{2,1,0:T(8,128)(2,1)S(1)}, bf16[2,128,256]{2,1,0:T(8,128)(2,1)S(1)}, u32[]{:S(2)}, u32[]{:S(2)}) %collective-permute-start.1) | collective-permute-done | bytes 131104 | tf_op jit(solution)/shard_map/ppermute | solution.py:15
  25.7 1.9 collective-permute-start.2
  27.5 2.4 fusion.13
  29.9 8.7 %collective-permute-done.2 = bf16[2,256,256]{2,1,0:T(8,128)(2,1)S(1)} collective-permute-done((bf16[2,256,256]{2,1,0:T(8,128)(2,1)S(1)}, bf16[2,256,256]{2,1,0:T(8,128)(2,1)S(1)}, u32[]{:S(2)}, u32[]{:S(2)}) %collective-permute-start.2) | collective-permute-done | bytes 262176 | tf_op jit(solution)/shard_map/ppermute | solution.py:15
  38.6 1.0 maximum_select_fusion.3
  39.6 2.7 %collective-permute-start.3 = (bf16[2,512,256]{2,1,0:T(8,128)(2,1)}, bf16[2,512,256]{2,1,0:T(8,128)(2,1)}, u32[]{:S(2)}, u32[]{:S(2)}) collective-permute-start(bf16[2,512,256]{2,1,0:T(8,128)(2,1)} %maximum_select_fusion.3), channel_id=1, source_target_pairs={{0,8},{1,9},{2,10},{3,11},{4,12},{5,13},{6,14},{7,15},{8,0},{9,1},... | collective-permute-start | bytes 1572872 | tf_op jit(solution)/shard_map/ppermute | solution.py:15
  42.2 1.4 fusion.16
  45.4 31.8 %collective-permute-done.3 = bf16[2,512,256]{2,1,0:T(8,128)(2,1)} collective-permute-done((bf16[2,512,256]{2,1,0:T(8,128)(2,1)}, bf16[2,512,256]{2,1,0:T(8,128)(2,1)}, u32[]{:S(2)}, u32[]{:S(2)}) %collective-permute-start.3) | collective-permute-done | bytes 524320 | tf_op jit(solution)/shard_map/ppermute | solution.py:15
  77.2 1.3 copy.25
  78.4 1.7 fusion.45
  80.2 1.3 copy-done.2
  82.1 4.7 %copy.27 = bf16[2,1024,768]{1,2,0:T(8,128)(2,1)} copy(bf16[2,1024,768]{2,1,0:T(8,128)(2,1)} %all-gather.5.cloned.1.call-done) | data formatting | bytes 6291456 | tf_op jit(solution)/shard_map/all_gather | solution.py:72
  86.8 3.7 %fusion.15 = bf16[2,64,4,192]{3,1,2,0:T(8,128)(2,1)S(1)} fusion(bf16[2,1024,4,192]{1,3,2,0:T(8,128)(2,1)} %bitcast.41, f32[2,4,64,1024]{3,2,1,0:T(8,128)} %copy-done.2, f32[2,4,64]{2,1,0:T(4,128)S(1)} %broadcast_maximum_fusion, f32[2,64,4]{1,2,0:T(4,128)S(1)} %bitcast.52), kind=kOutput, calls=%fused_computation.28 | convolution fusion | flops 202571776 | bytes 5443584 | tf_op jit(solution)/shard_map/shqk,skhv->shqv/dot_general | solution.py:80
  91.6 40.1 %all-gather.7.cloned.1.call-done = bf16[1536,1536]{1,0:T(8,128)(2,1)} async-done(((bf16[96,1536]{1,0:T(8,128)(2,1)}), bf16[1536,1536]{1,0:T(8,128)(2,1)}) %all-gather.7.cloned.1.call-update) | async-done | bytes 4718608 | tf_op jit(solution)/shard_map/all_gather | solution.py:44
  131.8 3.8 %convolution_convert_fusion.1 = bf16[128,1536]{1,0:T(8,128)(2,1)S(1)} fusion(bf16[1536,1536]{1,0:T(8,128)(2,1)} %all-gather.7.cloned.1.call-done, bf16[128,768]{1,0:T(8,128)(2,1)} %convert_element_type.71, bf16[768,1536]{1,0:T(8,128)(2,1)S(1)} %copy-done, bf16[128,1536]{1,0:T(8,128)(2,1)S(1)} %bitcast.40), kind=kOutput, calls=%fused_computation.6 | convolution fusion | flops 908722176 | bytes 8060928 | tf_op jit(solution)/shard_map/dot_general | solution.py:95
  135.6 1.6 broadcast_in_dim.5
  137.1 3.1 %convert_element_type.78 = f32[256,1536]{1,0:T(8,128)} reshape(f32[2,64,2,1536]{3,2,1,0:T(2,128)} %broadcast_in_dim.5) | data formatting | bytes 3145728 | tf_op jit(solution)/shard_map/convert_element_type | solution.py:105
  140.3 41.1 %all-gather.9.cloned.1.call-done = bf16[1280,1536]{1,0:T(8,128)(2,1)} async-done(((bf16[80,1536]{1,0:T(8,128)(2,1)}), bf16[1280,1536]{1,0:T(8,128)(2,1)}) %all-gather.9.cloned.1.call-update) | async-done | bytes 3932176 | tf_op jit(solution)/shard_map/all_gather | solution.py:45
  181.4 3.8 %fusion = bf16[256,1536]{1,0:T(8,128)(2,1)S(1)} fusion(f32[256,1536]{1,0:T(8,128)} %convert_element_type.78, bf16[256,1280]{1,0:T(8,128)(2,1)S(1)} %bitcast.47, bf16[1280,1536]{1,0:T(8,128)(2,1)} %all-gather.9.cloned.1.call-done), kind=kOutput, calls=%fused_computation.1 | convolution fusion | flops 1007419392 | bytes 6946816 | tf_op jit(solution)/shard_map/dot_general | solution.py:103
  185.2 2.2 collective-permute-start.4
  187.4 1.3 collective-permute-start.5
  188.8 1.7 collective-permute-done.5
  191.2 44.9 %all-gather.11.cloned.1.call-done = bf16[1536,1536]{0,1:T(8,128)(2,1)} async-done(((bf16[1536,96]{0,1:T(8,128)(2,1)}), bf16[1536,1536]{0,1:T(8,128)(2,1)}) %all-gather.11.cloned.1.call-update) | async-done | bytes 4718608 | tf_op jit(solution)/shard_map/all_gather | solution.py:46
  236.1 4.6 %convolution_convert_fusion = bf16[256,1536]{1,0:T(8,128)(2,1)} fusion(bf16[256,1536]{1,0:T(8,128)(2,1)S(1)} %bitcast.46, bf16[1536,1536]{0,1:T(8,128)(2,1)} %all-gather.11.cloned.1.call-done), kind=kOutput, calls=%fused_computation.2 | convolution fusion | flops 1208352768 | bytes 6291456 | tf_op jit(solution)/shard_map/dot_general | solution.py:117
  (42 shorter events, 7.8 us)
Async XLA Ops:
  6.5 125.2 %copy-start = (bf16[768,1536]{1,0:T(8,128)(2,1)S(1)}, bf16[768,1536]{1,0:T(8,128)(2,1)}, u32[]{:S(2)}) copy-start(bf16[768,1536]{1,0:T(8,128)(2,1)} %param.17) | copy-start | bytes 7077892
  6.5 75.6 %all-gather.5.cloned.1.call-start = ((), (), s32[]{:S(2)}) async-start(), calls=%async_computation | async-start | bytes 3342336 | tf_op jit(solution)/shard_map/all_gather | solution.py:72
  10.4 5.0 %copy-start.3 = (bf16[1536,256]{1,0:T(8,128)(2,1)S(1)}, bf16[1536,256]{1,0:T(8,128)(2,1)}, u32[]{:S(2)}) copy-start(bf16[1536,256]{1,0:T(8,128)(2,1)} %param.15) | copy-start | bytes 2359300
  13.3 118.5 %all-gather.7.cloned.1.call-start = ((), (), s32[]{:S(2)}) async-start(), calls=%async_computation.1 | async-start | bytes 5013504 | tf_op jit(solution)/shard_map/all_gather | solution.py:44
  14.1 167.4 %all-gather.9.cloned.1.call-start = ((), (), s32[]{:S(2)}) async-start(), calls=%async_computation.2 | async-start | bytes 4177920 | tf_op jit(solution)/shard_map/all_gather | solution.py:45
  14.8 221.3 %all-gather.11.cloned.1.call-start = ((), (), s32[]{:S(2)}) async-start(), calls=%async_computation.3 | async-start | bytes 5013504 | tf_op jit(solution)/shard_map/all_gather | solution.py:46
  16.3 1.6 collective-permute-start
  18.8 6.8 %collective-permute-start.1 = (bf16[2,128,256]{2,1,0:T(8,128)(2,1)S(1)}, bf16[2,128,256]{2,1,0:T(8,128)(2,1)S(1)}, u32[]{:S(2)}, u32[]{:S(2)}) collective-permute-start(bf16[2,128,256]{2,1,0:T(8,128)(2,1)S(1)} %maximum_select_fusion.7), channel_id=1, source_target_pairs={{0,2},{1,3},{2,0},{3,1},{4,6},{5,7},{6,4},{7,5},{8,10},{9,11},{10,... | collective-permute-start | bytes 393224 | tf_op jit(solution)/shard_map/ppermute | solution.py:15
  25.7 12.9 %collective-permute-start.2 = (bf16[2,256,256]{2,1,0:T(8,128)(2,1)S(1)}, bf16[2,256,256]{2,1,0:T(8,128)(2,1)S(1)}, u32[]{:S(2)}, u32[]{:S(2)}) collective-permute-start(bf16[2,256,256]{2,1,0:T(8,128)(2,1)S(1)} %maximum_select_fusion.5), channel_id=1, source_target_pairs={{0,4},{1,5},{2,6},{3,7},{4,0},{5,1},{6,2},{7,3},{8,12},{9,13},{10,... | collective-permute-start | bytes 786440 | tf_op jit(solution)/shard_map/ppermute | solution.py:15
  39.6 37.6 %collective-permute-start.3 = (bf16[2,512,256]{2,1,0:T(8,128)(2,1)}, bf16[2,512,256]{2,1,0:T(8,128)(2,1)}, u32[]{:S(2)}, u32[]{:S(2)}) collective-permute-start(bf16[2,512,256]{2,1,0:T(8,128)(2,1)} %maximum_select_fusion.3), channel_id=1, source_target_pairs={{0,8},{1,9},{2,10},{3,11},{4,12},{5,13},{6,14},{7,15},{8,0},{9,1},... | collective-permute-start | bytes 1572872 | tf_op jit(solution)/shard_map/ppermute | solution.py:15
  80.2 1.4 copy-start.2
  86.8 45.0 %copy-start.1 = (bf16[2,64,1536]{2,1,0:T(8,128)(2,1)S(1)}, bf16[2,64,1536]{2,1,0:T(8,128)(2,1)}, u32[]{:S(2)}) copy-start(bf16[2,64,1536]{2,1,0:T(8,128)(2,1)} %param.11) | copy-start | bytes 1179652
  135.6 45.8 %copy-start.4 = (bf16[2,128,1280]{2,1,0:T(8,128)(2,1)S(1)}, bf16[2,128,1280]{2,1,0:T(8,128)(2,1)}, u32[]{:S(2)}) copy-start(bf16[2,128,1280]{2,1,0:T(8,128)(2,1)} %fusion.13) | copy-start | bytes 1966084
  181.4 7.3 %copy-start.5 = (f32[3,1536]{1,0:T(4,128)S(1)}, f32[3,1536]{1,0:T(4,128)}, u32[]{:S(2)}) copy-start(f32[3,1536]{1,0:T(4,128)} %param.20) | copy-start | bytes 55300
  185.2 3.5 %collective-permute-start.4 = (bf16[2,1,1536]{2,1,0:T(2,128)(2,1)S(1)}, bf16[2,1,1536]{2,1,0:T(2,128)(2,1)S(1)}, u32[]{:S(2)}, u32[]{:S(2)}) collective-permute-start(bf16[2,1,1536]{2,1,0:T(2,128)(2,1)S(1)} %get-tuple-element.8), channel_id=1, source_target_pairs={{0,1},{1,2},{2,3},{3,4},{4,5},{5,6},{6,7},{7,8},{8,9},{9,10},{10,1... | collective-permute-start | bytes 18440 | tf_op jit(solution)/shard_map/ppermute | solution.py:31
  187.4 3.1 %collective-permute-start.5 = (bf16[2,1,1536]{2,1,0:T(2,128)(2,1)S(1)}, bf16[2,1,1536]{2,1,0:T(2,128)(2,1)S(1)}, u32[]{:S(2)}, u32[]{:S(2)}) collective-permute-start(bf16[2,1,1536]{2,1,0:T(2,128)(2,1)S(1)} %get-tuple-element.9), channel_id=1, source_target_pairs={{1,0},{2,1},{3,2},{4,3},{5,4},{6,5},{7,6},{8,7},{9,8},{10,9},{11,1... | collective-permute-start | bytes 18440 | tf_op jit(solution)/shard_map/ppermute | solution.py:33
Sparse Core Ops, SparseCore 0:
  13.4 60.0 all-gather.4
  75.8 55.8 all-gather.6
  134.0 47.3 all-gather.8
  183.6 52.4 all-gather.10
